TPU v7x, 128 devices: a whole 4x4x4 slice. The times are simulated.
128 devices in a mesh: pipe: 16 (over y, x_hi, core), tensor: 8 (over z, x_lo).
Axes of the slice: x: 4 (x_hi: 2, x_lo: 2; x = x_hi * 2 + x_lo), y: 4, z: 4, core: 2. Of those that a mesh axis runs over, the one named last changes fastest.
Arguments:
- forward_input: bfloat16 [16, 512, 4096], P('pipe'), may hold values from -6 to 6
- saved_input: bfloat16 [16, 512, 4096], P('pipe'), may hold values from -6 to 6
- gradient_input: bfloat16 [16, 512, 4096], P('pipe'), may hold values from -6 to 6
- roster: int32 [16, 2], P('pipe'), may hold values from 0 to 1
- sign_bits: int32 [4096], replicated, may hold values from 0 to 1
- gain: float32 [16, 2, 4096], P('pipe'), may hold values from 0.5 to 1.5
- w_query: bfloat16 [16, 2, 4096, 4096], P('pipe', None, None, 'tensor'), may hold values from -0.09375 to 0.09375
- w_key: bfloat16 [16, 2, 4096, 1024], P('pipe', None, None, 'tensor'), may hold values from -0.09375 to 0.09375
- w_value: bfloat16 [16, 2, 4096, 1024], P('pipe', None, None, 'tensor'), may hold values from -0.09375 to 0.09375
- w_out: bfloat16 [16, 2, 4096, 4096], P('pipe', None, 'tensor'), may hold values from -0.09375 to 0.09375
Outputs:
- next_activation: bfloat16 [16, 512, 4096], P('pipe')
- next_gradient: bfloat16 [16, 512, 4096], P('pipe')
All inputs are finite; a program needn't handle non-finite values.
Results may differ from a plain program's by a relative error of at most 0.015.
Values may be sent and summed in bfloat16 or wider, within the bound.
A program may use at most 192 MiB of HBM per device.

v0:
```python
import math
import jax
import jax.numpy as jnp
from jax import lax
from jax.sharding import PartitionSpec as P

HD = 128
HB = 128
eps = 1e-05


def shifted(value, axis, steps):
    count = lax.axis_size(axis)
    pairs = [(source, (source + steps) % count) for source in range(count)]
    return lax.ppermute(value, axis, pairs)


def hadamard(order):
    index = jnp.arange(order, dtype=jnp.int32)
    common = index[:, None] & index[None, :]
    parity = jnp.zeros((order, order), jnp.int32)
    for place in range(order.bit_length() - 1):
        parity = parity ^ common >> place & 1
    return (1 - 2 * parity).astype(jnp.float32)


def rotate(values, signs):
    count = values.shape[0]
    blocks = (values * signs).reshape(count, -1, HB)
    turned = jnp.einsum("rbk,kj->rbj", blocks, hadamard(HB), precision=lax.Precision.HIGHEST)
    return (turned / math.sqrt(HB)).reshape(count, -1)


def unrotate(values, signs):
    count = values.shape[0]
    blocks = values.astype(jnp.float32).reshape(count, -1, HB)
    turned = jnp.einsum("rbk,kj->rbj", blocks, hadamard(HB), precision=lax.Precision.HIGHEST)
    return (turned / math.sqrt(HB)).reshape(count, -1) * signs


def heads_part(inputs, gains, query_w, key_w, value_w, out_w):
    rows = inputs.shape[0]
    kv_count = key_w.shape[1] // HD
    q_count = query_w.shape[1] // HD
    group = q_count // kv_count
    scale = lax.rsqrt(jnp.mean(inputs * inputs, axis=-1, keepdims=True) + eps)
    normed = (inputs * scale * gains).astype(jnp.bfloat16)
    query = jnp.dot(normed, query_w, preferred_element_type=jnp.float32).astype(jnp.bfloat16)
    keys = jnp.dot(normed, key_w, preferred_element_type=jnp.float32).astype(jnp.bfloat16)
    values = jnp.dot(normed, value_w, preferred_element_type=jnp.float32).astype(jnp.bfloat16)
    query = query.reshape(rows, kv_count, group, HD).astype(jnp.float32)
    keys = keys.reshape(rows, kv_count, HD).astype(jnp.float32)
    values = values.reshape(rows, kv_count, HD).astype(jnp.float32)
    scores = jnp.einsum("qkgd,skd->kgqs", query, keys) / math.sqrt(HD)
    position = jnp.arange(rows, dtype=jnp.int32)
    allowed = position[:, None] >= position[None, :]
    scores = jnp.where(allowed, scores, -1e30)
    top = jnp.max(scores, axis=-1, keepdims=True)
    expo = jnp.exp(scores - top)
    probs = (expo / jnp.sum(expo, axis=-1, keepdims=True)).astype(jnp.bfloat16)
    context = jnp.einsum("kgqs,skd->qkgd", probs.astype(jnp.float32), values).astype(jnp.bfloat16)
    context = context.reshape(rows, q_count * HD)
    return jnp.dot(context, out_w, preferred_element_type=jnp.float32)


def pick(stack, which):
    return lax.dynamic_index_in_dim(stack[0], which, 0, keepdims=False)


def local(
    forward_input,
    saved_input,
    gradient_input,
    roster,
    sign_bits,
    gain,
    w_query,
    w_key,
    w_value,
    w_out,
):
    signs = (2 * sign_bits - 1).astype(jnp.float32)
    front = roster[0, 0]
    back = roster[0, 1]
    front_w = (pick(w_query, front), pick(w_key, front), pick(w_value, front), pick(w_out, front))
    back_w = (pick(w_query, back), pick(w_key, back), pick(w_value, back), pick(w_out, back))
    gain_front = pick(gain, front)
    gain_back = pick(gain, back)
    inputs = unrotate(forward_input[0], signs)
    grad = unrotate(gradient_input[0], signs)
    stored = saved_input[0].astype(jnp.float32)
    partial_out = heads_part(inputs, gain_front, *front_w)
    _, pull = jax.vjp(lambda v: heads_part(v, gain_back, *back_w), stored)
    partial_back = pull(grad)[0]
    mixed = lax.psum(partial_out.astype(jnp.bfloat16), "tensor").astype(jnp.float32)
    sent_activation = rotate(inputs + mixed, signs).astype(jnp.bfloat16)
    arrived = shifted(sent_activation, "pipe", 1)
    pulled = lax.psum(partial_back.astype(jnp.bfloat16), "tensor").astype(jnp.float32)
    sent_gradient = rotate(grad + pulled, signs).astype(jnp.bfloat16)
    returned = shifted(sent_gradient, "pipe", -1)
    return (arrived[None], returned[None])


def solution(mesh):
    placed = (
        P("pipe", None, None),
        P("pipe", None, None),
        P("pipe", None, None),
        P("pipe", None),
        P(),
        P("pipe", None, None),
        P("pipe", None, None, "tensor"),
        P("pipe", None, None, "tensor"),
        P("pipe", None, None, "tensor"),
        P("pipe", None, "tensor", None),
    )
    return jax.shard_map(
        local,
        mesh=mesh,
        in_specs=placed,
        out_specs=(P("pipe", None, None), P("pipe", None, None)),
        check_vma=False,
    )
```

profile of v0, /device:TPU:1, one launch (start us, length us, event | category | flops | bytes accessed | tf_op | source)
XLA Modules:
  0.0 628.2 jit_solution(7239126787473838234)
XLA Ops:
  19.5 4.9 fusion.71
  27.9 7.8 %multiply_reduce_fusion = (f32[512]{0:T(512)S(1)}, f32[128,512,32]{1,0,2:T(8,128)S(1)}) fusion(f32[32,128]{1,0:T(8,128)S(1)} %multiply_bitcast_fusion.2, bf16[512,32,128]{2,1,0:T(8,128)(2,1)S(1)} %bitcast.297), kind=kOutput, calls=%fused_computation.27 | convolution fusion | flops 3227909632 | bytes 12601344 | tf_op jit(solution)/shard_map/rbk,kj->rbj/dot_general | solution.py:37
  47.0 10.1 %bitcast_multiply_fusion = (bf16[512,32,128]{0,2,1:T(8,128)(2,1)S(1)}, f32[128,512,32]{1,0,2:T(8,128)}) fusion(f32[32,128]{1,0:T(8,128)S(1)} %multiply_bitcast_fusion.2, bf16[512,32,128]{2,1,0:T(8,128)(2,1)S(1)} %bitcast.294), kind=kOutput, calls=%fused_computation.17 | convolution fusion | flops 3225812992 | bytes 16793600 | tf_op jit(solution)/shard_map/rbk,kj->rbj/dot_general | solution.py:37
  60.3 6.9 %convolution_convert_fusion.4 = bf16[4,512,512]{1,2,0:T(8,128)(2,1)} fusion(bf16[128,4,512]{2,0,1:T(8,128)(2,1)} %bitcast.317, bf16[1,2,4096,128]{3,2,1,0:T(8,128)(2,1)} %param.18, s32[]{:T(128)S(6)} %select_n.32, bf16[1,512,4096]{2,1,0:T(8,128)(2,1)} %param.11, f32[4096]{0:T(1024)S(1)} %bitcast.309, f32[512]{0:T(512)S(1)} %fusion.149), kind=kOutput, calls=%fused_computation.89 | convolution fusion | flops 814809088 | bytes 7882756 | tf_op jit(solution)/shard_map/transpose(jvp(kgqs,skd->qkgd))/dot_general | solution.py:61
  67.2 8.8 %convert_reduce_fusion = (f32[4,512]{1,0:T(4,128)S(1)}, pred[1,4,512,512]{2,3,1,0:T(32,128)(4,1)}, f32[4,512]{1,0:T(4,128)S(1)}, f32[4,512]{1,0:T(4,128)S(1)}, f32[512,512,4]{1,0,2:T(8,128)}) fusion(f32[4,512]{1,0:T(4,128)S(1)} %get-tuple-element.20, f32[512,512,4]{1,0,2:T(8,128)} %copy-done.2, pred[512,512]{0,1:T(8,128)(4,1)S(1)} %iota_compare_fusion, ...), kind=kOutput, calls=%fused_computation.62 | convolution fusion | flops 818997248 | bytes 17604612 | tf_op jit(solution)/shard_map/qkgd,skd->kgqs/dot_general | solution.py:54
  76.0 5.4 fusion.189
  85.6 9.2 %convolution_convert_fusion = bf16[512,4096]{1,0:T(8,128)(2,1)} fusion(bf16[512,4,128]{0,2,1:T(8,128)(2,1)S(1)} %bitcast.306, pred[1,4,512,512]{2,3,1,0:T(32,128)(4,1)} %get-tuple-element.9, f32[4,512]{1,0:T(4,128)S(1)} %negate_divide_fusion, pred[512,512]{0,1:T(8,128)(4,1)S(1)} %iota_compare_fusion, bf16[1,2,4096,128]{3,2,1,0:T(8,128)(2,1)S(1)} %copy-done, ...), kind=kOutput, calls=%fused_computation.28 | convolution fusion | flops 819003392 | bytes 13402116 | tf_op jit(solution)/shard_map/transpose(jvp())/dot_general | solution.py:49
  94.8 5.8 fusion.77
  100.7 6.6 %convolution_convert_fusion.3 = bf16[512,4096]{1,0:T(8,128)(2,1)} fusion(bf16[512,512]{0,1:T(8,128)(2,1)S(1)} %bitcast.321, bf16[1,2,512,4096]{3,2,1,0:T(8,128)(2,1)} %param.19, s32[]{:T(128)S(6)} %select_n.30), kind=kOutput, calls=%fused_computation.31 | convolution fusion | flops 2149580800 | bytes 8912900 | tf_op jit(solution)/shard_map/dot_general | solution.py:63
  107.3 6.8 %convolution_convert_fusion.2 = bf16[512,4096]{1,0:T(8,128)(2,1)} fusion(bf16[512,512]{0,1:T(8,128)(2,1)S(1)} %bitcast.320, bf16[1,2,4096,512]{3,2,1,0:T(8,128)(2,1)} %param.16, s32[]{:T(128)S(6)} %select_n.32), kind=kOutput, calls=%fused_computation.30 | convolution fusion | flops 2149580800 | bytes 8912900 | tf_op jit(solution)/shard_map/transpose(jvp())/dot_general | solution.py:48
  114.1 11.8 %fusion.4 = (f32[512]{0:T(512)S(1)}, bf16[512,4096]{1,0:T(8,128)(2,1)}) fusion(bf16[1,512,4096]{2,1,0:T(8,128)(2,1)} %param.11, f32[4096]{0:T(1024)S(1)} %bitcast.310, bf16[512,4096]{1,0:T(8,128)(2,1)} %convolution_convert_fusion.2, bf16[512,4096]{1,0:T(8,128)(2,1)} %convolution_convert_fusion, bf16[1,2,4096,128]{3,2,1,0:T(8,128)(2,1)S(1)} %copy-done.11, ...), kind=kOutput, calls=%fused_computation.7 | convolution fusion | flops 835780096 | bytes 22841348 | tf_op jit(solution)/shard_map/transpose(jvp())/dot_general | solution.py:50
  125.9 6.1 fusion.7
  132.0 9.0 %copy.13 = f32[512,4096]{1,0:T(8,128)} copy(f32[512,4096]{0,1:T(8,128)} %bitcast.292) | data formatting | bytes 16777216 | tf_op jit(solution)/shard_map/reshape | solution.py:38
  141.0 8.3 %bitcast_multiply_fusion.1 = f32[512,32,128]{0,2,1:T(8,128)} fusion(f32[128,512,32]{1,0,2:T(8,128)} %get-tuple-element.25), kind=kLoop, calls=%fused_computation.18 | loop fusion | flops 2097152 | bytes 16777216 | tf_op jit(solution)/shard_map/div | solution.py:38
  149.3 9.0 %copy.19 = f32[512,4096]{1,0:T(8,128)} copy(f32[512,4096]{0,1:T(8,128)} %bitcast.293) | data formatting | bytes 16777216 | tf_op jit(solution)/shard_map/reshape | solution.py:38
  158.2 317.3 %all-reduce.3.cloned.1.call-done = (bf16[512,4096]{1,0:T(8,128)(2,1)}, bf16[512,4096]{1,0:T(8,128)(2,1)}) async-done(((bf16[512,4096]{1,0:T(8,128)(2,1)}, bf16[512,4096]{1,0:T(8,128)(2,1)}), (bf16[512,4096]{1,0:T(8,128)(2,1)}, bf16[512,4096]{1,0:T(8,128)(2,1)})) %all-reduce.3.cloned.1.call-update) | async-done | bytes 8388624 | tf_op jit(solution)/shard_map/psum | solution.py:95
  475.6 13.6 %multiply_bitcast_fusion = (f32[64,32,8,128]{3,2,1,0:T(8,128)}, f32[64,32,8,128]{3,2,1,0:T(8,128)S(1)}) fusion(bf16[512,4096]{1,0:T(8,128)(2,1)} %get-tuple-element.7, f32[512,4096]{1,0:T(8,128)} %copy.19, f32[4096]{0:T(1024)S(1)} %add_convert_fusion, bf16[512,4096]{1,0:T(8,128)(2,1)} %get-tuple-element.6, f32[512,4096]{1,0:T(8,128)} %copy.13), kind=kLoop, calls=%fused_computation.22 | loop fusion | flops 16777216 | bytes 41959424
  489.2 13.2 %multiply_convert_fusion = bf16[512,32,128]{0,2,1:T(8,128)(2,1)} fusion(f32[64,32,8,128]{3,2,1,0:T(8,128)} %get-tuple-element.16), kind=kOutput, calls=%fused_computation.21 | convolution fusion | flops 3225812992 | bytes 12582912 | tf_op jit(solution)/shard_map/rbk,kj->rbj/dot_general | solution.py:30
  502.4 9.7 %multiply_convert_fusion.1 = bf16[512,32,128]{0,2,1:T(8,128)(2,1)} fusion(f32[64,32,8,128]{3,2,1,0:T(8,128)S(1)} %get-tuple-element.17), kind=kOutput, calls=%fused_computation.24 | convolution fusion | flops 3225812992 | bytes 12582912 | tf_op jit(solution)/shard_map/rbk,kj->rbj/dot_general | solution.py:30
  512.2 6.3 %copy.17 = bf16[512,4096]{1,0:T(8,128)(2,1)} copy(bf16[512,4096]{0,1:T(8,128)(2,1)} %bitcast.296) | data formatting | bytes 8388608 | tf_op jit(solution)/shard_map/convert_element_type | solution.py:96
  521.5 6.3 %copy.24 = bf16[512,4096]{1,0:T(8,128)(2,1)} copy(bf16[512,4096]{0,1:T(8,128)(2,1)} %bitcast.295) | data formatting | bytes 8388608 | tf_op jit(solution)/shard_map/convert_element_type | solution.py:99
  527.8 74.7 %collective-permute-done = bf16[512,4096]{1,0:T(8,128)(2,1)} collective-permute-done((bf16[512,4096]{1,0:T(8,128)(2,1)}, bf16[512,4096]{1,0:T(8,128)(2,1)}, u32[]{:S(2)}, u32[]{:S(2)}) %collective-permute-start) | collective-permute-done | bytes 4194336 | tf_op jit(solution)/shard_map/ppermute | solution.py:15
  602.5 11.5 %collective-permute-done.1 = bf16[512,4096]{1,0:T(8,128)(2,1)S(1)} collective-permute-done((bf16[512,4096]{1,0:T(8,128)(2,1)}, bf16[512,4096]{1,0:T(8,128)(2,1)S(1)}, u32[]{:S(2)}, u32[]{:S(2)}) %collective-permute-start.1) | collective-permute-done | bytes 4194336 | tf_op jit(solution)/shard_map/ppermute | solution.py:15
  614.0 4.8 copy.62
  (66 shorter events, 35.4 us)
Async XLA Ops:
  7.2 8.6 %copy-start = (bf16[1,2,4096,128]{3,2,1,0:T(8,128)(2,1)S(1)}, bf16[1,2,4096,128]{3,2,1,0:T(8,128)(2,1)}, u32[]{:S(2)}) copy-start(bf16[1,2,4096,128]{3,2,1,0:T(8,128)(2,1)} %param.17) | copy-start | bytes 6291460
  7.2 7.2 %copy-start.9 = (s32[4096]{0:T(1024)S(1)}, s32[4096]{0:T(1024)}, u32[]{:S(2)}) copy-start(s32[4096]{0:T(1024)} %param.14) | copy-start | bytes 49156
  7.2 8.5 %copy-start.10 = (f32[1,2,4096]{2,1,0:T(2,128)S(1)}, f32[1,2,4096]{2,1,0:T(2,128)}, u32[]{:S(2)}) copy-start(f32[1,2,4096]{2,1,0:T(2,128)} %param.15) | copy-start | bytes 98308
  7.2 468.4 %all-reduce.3.cloned.1.call-start = ((), (), s32[]{:S(2)}) async-start(), calls=%async_computation | async-start | bytes 16777216 | tf_op jit(solution)/shard_map/psum | solution.py:95
  15.8 3.7 copy-start.4
  19.5 4.9 copy-start.5
  24.4 2.2 copy-start.6
  27.9 12.1 %slice-start.2 = ((s8[8388608]{0:T(1024)(128)(4,1)}), s8[4194304]{0:T(1024)(128)(4,1)S(1)}, s32[]{:S(2)}) async-start(s8[8388608]{0:T(1024)(128)(4,1)} %bitcast.315), calls=%async_computation.3 | async-start | bytes 8388608
  35.7 4.2 slice-start.3
  39.9 3.2 copy-start.7
  44.0 2.0 copy-start.2
  46.0 11.1 %slice-start = ((s8[8388608]{0:T(1024)(128)(4,1)}), s8[4194304]{0:T(1024)(128)(4,1)S(1)}, s32[]{:S(2)}) async-start(s8[8388608]{0:T(1024)(128)(4,1)} %bitcast.313), calls=%async_computation.1 | async-start | bytes 8388608
  47.0 10.2 %slice-start.1 = ((s8[8388608]{0:T(1024)(128)(4,1)}), s8[4194304]{0:T(1024)(128)(4,1)S(1)}, s32[]{:S(2)}) async-start(s8[8388608]{0:T(1024)(128)(4,1)} %bitcast.313), calls=%async_computation.2 | async-start | bytes 8388608
  76.0 5.4 copy-start.3
  76.0 5.9 copy-start.8
  76.0 6.1 copy-start.14
  100.7 6.6 %copy-start.13 = (bf16[512,4,128]{0,2,1:T(8,128)(2,1)S(1)}, bf16[512,4,128]{0,2,1:T(8,128)(2,1)}, u32[]{:S(2)}) copy-start(bf16[512,4,128]{0,2,1:T(8,128)(2,1)} %fusion.74) | copy-start | bytes 1572868
  107.3 6.8 %copy-start.11 = (bf16[1,2,4096,128]{3,2,1,0:T(8,128)(2,1)S(1)}, bf16[1,2,4096,128]{3,2,1,0:T(8,128)(2,1)}, u32[]{:S(2)}) copy-start(bf16[1,2,4096,128]{3,2,1,0:T(8,128)(2,1)} %param.18) | copy-start | bytes 6291460
  107.3 6.8 %copy-start.12 = (bf16[512,512]{0,1:T(8,128)(2,1)S(1)}, bf16[512,512]{0,1:T(8,128)(2,1)}, u32[]{:S(2)}) copy-start(bf16[512,512]{0,1:T(8,128)(2,1)} %fusion.68) | copy-start | bytes 1572868
  518.5 84.1 %collective-permute-start = (bf16[512,4096]{1,0:T(8,128)(2,1)}, bf16[512,4096]{1,0:T(8,128)(2,1)}, u32[]{:S(2)}, u32[]{:S(2)}) collective-permute-start(bf16[512,4096]{1,0:T(8,128)(2,1)} %copy.17), channel_id=1, source_target_pairs={{0,8},{8,16},{16,24},{24,32},{32,40},{40,48},{48,56},{56,64},{64,7... | collective-permute-start | bytes 12582920 | tf_op jit(solution)/shard_map/ppermute | solution.py:15
  527.8 86.2 %collective-permute-start.1 = (bf16[512,4096]{1,0:T(8,128)(2,1)}, bf16[512,4096]{1,0:T(8,128)(2,1)S(1)}, u32[]{:S(2)}, u32[]{:S(2)}) collective-permute-start(bf16[512,4096]{1,0:T(8,128)(2,1)} %copy.24), channel_id=1, source_target_pairs={{0,120},{8,0},{16,8},{24,16},{32,24},{40,32},{48,40},{56,48},{64,5... | collective-permute-start | bytes 12582920 | tf_op jit(solution)/shard_map/ppermute | solution.py:15
  614.0 6.9 %copy-start.1 = (bf16[1,2,4096,128]{3,2,1,0:T(8,128)(2,1)S(1)}, bf16[1,2,4096,128]{3,2,1,0:T(8,128)(2,1)}, u32[]{:S(2)}) copy-start(bf16[1,2,4096,128]{3,2,1,0:T(8,128)(2,1)} %param.17) | copy-start | bytes 6291460
Sparse Core Ops, SparseCore 0:
  132.1 343.3 all-reduce.2
where the time goes:
time: 638 us; the launch traced here: 628 us
  waiting for transfers between devices  404 us (63%)
  matrix products  116 us (18%)
  local copies, waits for them, and re-layouts  45.1 us (7%)
  other arithmetic  41.7 us (7%)
  between operations  18.7 us (3%)
    psum x1, waiting for transfers between devices, local(): lax.psum(partial_out.astype(jnp.bfloat16), 'tensor').astype(jnp.float32)  317 us
    ppermute x2, waiting for transfers between devices, shifted(): return lax.ppermute(value, axis, pairs)  86.2 us
    dot_general x2, matrix products, rotate(): jnp.einsum('rbk,kj->rbj', blocks, hadamard(HB), precision=lax.Precision.H...  23 us
    dot_general x2, matrix products, unrotate(): jnp.einsum('rbk,kj->rbj', blocks, hadamard(HB), precision=lax.Precision.H...  18 us
    reshape x2, local copies, waits for them, and re-layouts, unrotate(): return (turned / math.sqrt(HB)).reshape(count, -1) * signs  17.9 us
    dot_general x3, matrix products, heads_part(): jnp.dot(normed, query_w, preferred_element_type=jnp.float32)  14.9 us
    unnamed x3, other arithmetic  13.6 us
    dot_general x3, matrix products, heads_part(): scores = jnp.einsum('qkgd,skd->kgqs', query, keys) / math.sqrt(HD)  13.1 us
  transfers between devices with their start and end apart: 3, of which 3 were waited for; matrix products, arithmetic and copies ran while one was open for 5% of the time, Pallas kernels for 0%

commit v1 on v0

--- a/solution.py
+++ b/solution.py
@@ -92,7 +92,9 @@
     partial_out = heads_part(inputs, gain_front, *front_w)
     _, pull = jax.vjp(lambda v: heads_part(v, gain_back, *back_w), stored)
     partial_back = pull(grad)[0]
-    mixed = lax.psum(partial_out.astype(jnp.bfloat16), "tensor").astype(jnp.float32)
+    mixed = jnp.sum(lax.all_gather(partial_out.astype(jnp.bfloat16), "tensor"), axis=0).astype(
+        jnp.float32
+    )
     sent_activation = rotate(inputs + mixed, signs).astype(jnp.bfloat16)
     arrived = shifted(sent_activation, "pipe", 1)
     pulled = lax.psum(partial_back.astype(jnp.bfloat16), "tensor").astype(jnp.float32)

time: 638 us -> 1110 us (1.74)
  waiting for transfers between devices: 404 us -> 867 us
    all_gather x0 -> x1, waiting for transfers between devices: none -> 664 us  [local(): lax.all_gather(partial_out.astype(jnp.bfloat16), 'tensor')]
    psum x1, waiting for transfers between devices: 317 us -> 157 us  [local(): lax.psum(partial_back.astype(jnp.bfloat16), 'tensor').astype(jnp.float32)]
    ppermute x2, waiting for transfers between devices: 86.2 us -> 45.8 us  [shifted(): return lax.ppermute(value, axis, pairs)]
    reduce_sum x0 -> x1, other arithmetic: none -> 14.4 us  [local(): jnp.sum(lax.all_gather(partial_out.astype(jnp.bfloat16), 'tensor'), axis=0)]
    unnamed x3 -> x1, other arithmetic: 13.6 us -> 0.01 us
  transfers between devices with their start and end apart: 3 -> 4, of which waited for: 3 -> 3; matrix products, arithmetic and copies ran while one was open for 5% -> 9% of each run, Pallas kernels for 0% -> 0%
where the time goes in v1:
time: 1110 us; the launch traced here: 1100 us
  waiting for transfers between devices  867 us (78%)
  matrix products  125 us (11%)
  local copies, waits for them, and re-layouts  46.1 us (4%)
  other arithmetic  40.2 us (4%)
  between operations  18.6 us (2%)
    all_gather x1, waiting for transfers between devices, local(): lax.all_gather(partial_out.astype(jnp.bfloat16), 'tensor')  664 us
    psum x1, waiting for transfers between devices, local(): lax.psum(partial_back.astype(jnp.bfloat16), 'tensor').astype(jnp.float32)  157 us
    ppermute x2, waiting for transfers between devices, shifted(): return lax.ppermute(value, axis, pairs)  45.8 us
    dot_general x2, matrix products, rotate(): jnp.einsum('rbk,kj->rbj', blocks, hadamard(HB), precision=lax.Precision.H...  30.1 us
  transfers between devices with their start and end apart: 4, of which 3 were waited for; matrix products, arithmetic and copies ran while one was open for 9% of the time, Pallas kernels for 0%

profile of v1, /device:TPU:1, one launch (start us, length us, event | category | flops | bytes accessed | tf_op | source)
XLA Modules:
  0.0 1101.0 jit_solution(4065461815899490227)
XLA Ops:
  15.8 6.1 fusion.73
  30.5 9.9 bitcast_multiply_fusion
  40.4 7.4 multiply_reduce_fusion
  61.7 6.9 convolution_convert_fusion.4
  68.6 8.8 convert_reduce_fusion
  77.4 5.4 fusion.192
  82.8 9.2 convolution_convert_fusion
  92.1 5.6 fusion.76
  97.8 6.8 convolution_convert_fusion.2
  104.6 11.6 %fusion.4 = (f32[512]{0:T(512)S(1)}, bf16[512,4096]{1,0:T(8,128)(2,1)}) fusion(bf16[1,512,4096]{2,1,0:T(8,128)(2,1)} %param.11, f32[4096]{0:T(1024)S(1)} %bitcast.312, bf16[512,4096]{1,0:T(8,128)(2,1)} %convolution_convert_fusion.2, bf16[512,4096]{1,0:T(8,128)(2,1)} %convolution_convert_fusion, bf16[1,2,4096,128]{3,2,1,0:T(8,128)(2,1)S(1)} %copy-done.10, ...), kind=kOutput, calls=%fused_computation.7 | convolution fusion | flops 835780096 | bytes 22841348 | tf_op jit(solution)/shard_map/transpose(jvp())/dot_general | solution.py:50
  116.2 6.2 fusion.7
  122.5 5.5 fusion.79
  128.0 6.6 convolution_convert_fusion.3
  134.6 8.3 bitcast_multiply_fusion.1
  142.9 9.0 copy.31
  151.9 156.7 %all-reduce.2.cloned.1.call-done = bf16[512,4096]{1,0:T(8,128)(2,1)} async-done(((bf16[512,4096]{1,0:T(8,128)(2,1)}), bf16[512,4096]{1,0:T(8,128)(2,1)}) %all-reduce.2.cloned.1.call-update) | async-done | bytes 4194320 | tf_op jit(solution)/shard_map/psum | solution.py:100
  308.6 15.8 %multiply_convert_fusion = bf16[512,32,128]{0,2,1:T(8,128)(2,1)} fusion(bf16[512,4096]{1,0:T(8,128)(2,1)} %all-reduce.2.cloned.1.call-done, f32[512,4096]{1,0:T(8,128)} %copy.31, f32[4096]{0:T(1024)S(1)} %get-tuple-element.12), kind=kOutput, calls=%fused_computation.17 | convolution fusion | flops 3234201600 | bytes 16793600 | tf_op jit(solution)/shard_map/rbk,kj->rbj/dot_general | solution.py:30
  324.4 6.4 copy.36
  331.6 664.4 %all-gather.3.cloned.1.call-done = bf16[4096,4096]{1,0:T(8,128)(2,1)} async-done(((bf16[512,4096]{1,0:T(8,128)(2,1)}), bf16[4096,4096]{1,0:T(8,128)(2,1)}) %all-gather.3.cloned.1.call-update) | async-done | bytes 33554448 | tf_op jit(solution)/shard_map/all_gather | solution.py:95
  996.1 14.4 %reduce_sum.98 = bf16[512,4096]{1,0:T(8,128)(2,1)} reduce(bf16[8,512,4096]{2,1,0:T(8,128)(2,1)} %bitcast.294, bf16[]{:T(256)} %constant.85.clone.1), dimensions={0}, to_apply=%region_3.4 | reduce | flops 14680064 | bytes 37748736 | tf_op jit(solution)/shard_map/reduce_sum | solution.py:95
  1010.4 7.1 copy.27
  1017.5 14.3 %multiply_convert_fusion.1 = bf16[512,32,128]{0,2,1:T(8,128)(2,1)} fusion(f32[512,32,128]{0,2,1:T(8,128)} %bitcast.293, f32[128,512,32]{1,0,2:T(8,128)} %copy-done.2, f32[32,128]{1,0:T(8,128)S(1)} %get-tuple-element.13, f32[32,128]{1,0:T(8,128)S(1)} %broadcast_multiply_fusion), kind=kOutput, calls=%fused_computation.20 | convolution fusion | flops 3232104448 | bytes 21004288 | tf_op jit(solution)/shard_map/rbk,kj->rbj/dot_general | solution.py:30
  1031.8 6.3 copy.29
  1041.1 45.8 %collective-permute-done = bf16[512,4096]{1,0:T(8,128)(2,1)S(1)} collective-permute-done((bf16[512,4096]{1,0:T(8,128)(2,1)}, bf16[512,4096]{1,0:T(8,128)(2,1)S(1)}, u32[]{:S(2)}, u32[]{:S(2)}) %collective-permute-start) | collective-permute-done | bytes 4194336 | tf_op jit(solution)/shard_map/ppermute | solution.py:15
  (58 shorter events, 37.9 us)
Async XLA Ops:
  7.2 14.7 %copy-start = (bf16[1,2,4096,128]{3,2,1,0:T(8,128)(2,1)S(1)}, bf16[1,2,4096,128]{3,2,1,0:T(8,128)(2,1)}, u32[]{:S(2)}) copy-start(bf16[1,2,4096,128]{3,2,1,0:T(8,128)(2,1)} %param.17) | copy-start | bytes 6291460
  7.2 8.5 copy-start.9
  7.2 301.4 %all-reduce.2.cloned.1.call-start = ((), (), s32[]{:S(2)}) async-start(), calls=%async_computation | async-start | bytes 8388608 | tf_op jit(solution)/shard_map/psum | solution.py:100
  15.8 6.1 copy-start.4
  23.2 3.8 copy-start.8
  23.2 3.8 copy-start.5
  24.1 2.0 copy-start.3
  27.1 2.2 copy-start.6
  40.4 11.7 %slice-start = ((s8[8388608]{0:T(1024)(128)(4,1)}), s8[4194304]{0:T(1024)(128)(4,1)S(1)}, s32[]{:S(2)}) async-start(s8[8388608]{0:T(1024)(128)(4,1)} %bitcast.315), calls=%async_computation.2 | async-start | bytes 8388608
  47.8 4.3 copy-start.2
  47.8 5.3 slice-start.1
  52.1 4.3 copy-start.7
  97.7 6.8 copy-start.10
  97.7 6.8 copy-start.11
  122.5 873.6 %all-gather.3.cloned.1.call-start = ((), (), s32[]{:S(2)}) async-start(), calls=%async_computation.1 | async-start | bytes 37748736 | tf_op jit(solution)/shard_map/all_gather | solution.py:95
  330.8 710.3 %collective-permute-start.1 = (bf16[512,4096]{1,0:T(8,128)(2,1)}, bf16[512,4096]{1,0:T(8,128)(2,1)}, u32[]{:S(2)}, u32[]{:S(2)}) collective-permute-start(bf16[512,4096]{1,0:T(8,128)(2,1)} %copy.36), channel_id=1, source_target_pairs={{0,120},{8,0},{16,8},{24,16},{32,24},{40,32},{48,40},{56,48},{64,5... | collective-permute-start | bytes 12582920 | tf_op jit(solution)/shard_map/ppermute | solution.py:15
  1038.2 48.7 %collective-permute-start = (bf16[512,4096]{1,0:T(8,128)(2,1)}, bf16[512,4096]{1,0:T(8,128)(2,1)S(1)}, u32[]{:S(2)}, u32[]{:S(2)}) collective-permute-start(bf16[512,4096]{1,0:T(8,128)(2,1)} %copy.29), channel_id=1, source_target_pairs={{0,8},{8,16},{16,24},{24,32},{32,40},{40,48},{48,56},{56,64},{64,7... | collective-permute-start | bytes 12582920 | tf_op jit(solution)/shard_map/ppermute | solution.py:15
  1086.9 6.9 copy-start.1
Sparse Core Ops, SparseCore 0:
  122.6 185.9 all-reduce.1
  310.8 685.1 all-gather.2
